TPU v7x, 128 devices: a whole 4x4x4 slice. The times are simulated.
128 devices in a mesh: gx: 4 (over y), gy: 32 (over z, x, core).
Axes of the slice: x: 4, y: 4, z: 4, core: 2. Of those that a mesh axis runs over, the one named last changes fastest.
Arguments:
- fields: float32 [10, 64, 2048, 128], P(None, 'gx', 'gy'), may hold values from -6 to 6
- diffusivity: float32 [10], replicated, may hold values from 0.03 to 0.12
- decay_rates: float32 [10], replicated, may hold values from 0.3 to 1
- reaction_matrix: float32 [10, 10], replicated, may hold values from -1 to 1
- owner_index: int32 [4, 32768, 1], P('gx', 'gy'), may hold values from 0 to 31, as said below
- flame_flag: int32 [4, 32768, 1], P('gx', 'gy'), may hold values from 0 to 1, as said below
Outputs:
- new_fields: float32 [10, 64, 2048, 128], P(None, 'gx', 'gy')
- owner_heat: float32 [4, 32], P('gx', 'gy')
Inputs may be any that keep to these rules, and one draw needn't show every extreme that they name: `flame_flag`: each device holds exactly 256 or 32 flame blocks; in each index of gx exactly 4 devices along gy, consecutive with wraparound from a drawn start, hold 256. `owner_index`: the flame blocks of one index of gx, taken in order of device and then block, are dealt to owners in turn from a drawn first owner; so one device names each owner for at most 8 of its flame blocks and each owner receives at most 60 flame blocks, both bounds reached on every draw; a block outside the flame names its own device's index along gy.
All inputs are finite; a program needn't handle non-finite values.
Results may differ from a plain program's by a relative error of at most 0.0003.
Values sent between devices are 32-bit elements; how exact they have to be, the bound alone decides.
A program may use at most 128 MiB of HBM per device.

v0:
```python
import functools
import math

import jax
import jax.numpy as jnp
from jax import lax
from jax.experimental import pallas as pl
from jax.experimental.pallas import tpu as pltpu
from jax.sharding import PartitionSpec as P

H_STEP = 0.2
FLAME_SUB = 10
COMP = 10
CX, CY, CZ = 16, 64, 128
CH = CX * CY
FMAX = 256
RMAX = 60
GROUP = 2

F32, BF16 = jnp.float32, jnp.bfloat16
MESH = pl.DeviceIdType.MESH
VMEM = pl.BlockSpec(memory_space=pltpu.VMEM)
SMEM = pl.BlockSpec(memory_space=pltpu.SMEM)
ANY = pl.BlockSpec(memory_space=pl.ANY)
LIMIT = 56 << 20


def split(values):
    high = values.astype(BF16)
    low = (values - high.astype(F32)).astype(BF16)
    return high, low


def tables(reaction, decay, flags, owners, taps, matrix, inverse, lists, pad):
    exact = lax.Precision.HIGHEST
    iota = lax.broadcasted_iota
    one = jnp.float32(1.0)
    gap = jnp.abs((iota(jnp.int32, (2 * CZ, CZ), 0) & (CZ - 1)) - iota(jnp.int32, (2 * CZ, CZ), 1))
    taps[...] = jnp.where(gap == 0, -6.0, jnp.where(gap == 1, 1.0, 0.0)).astype(BF16)

    shares = [one / (one + H_STEP * jnp.full((8, CZ), decay[c], F32)) for c in range(COMP)]
    for c in range(COMP):
        inverse[pl.ds(8 * c, 8), :] = shares[c]
    sub, lane = iota(jnp.int32, (16, CZ), 0), iota(jnp.int32, (16, CZ), 1)
    by_row = jnp.zeros((16, CZ), F32)
    by_lane = jnp.zeros((16, CZ), F32)
    for c in range(COMP):
        share = jnp.concatenate([shares[c], shares[c]], axis=0)
        by_row = jnp.where(sub == c, share, by_row)
        by_lane = jnp.where(lane == c, share, by_lane)
    pad[...] = jnp.zeros((CZ, CZ), F32)
    pad[0:COMP, 0:COMP] = reaction[...]
    m1 = H_STEP * pad[0:16, :] * by_row
    pad[0:16, :] = m1
    full = pad[...]
    m2 = jnp.dot(m1, full, precision=exact, preferred_element_type=F32)
    m3 = jnp.dot(m2, full, precision=exact, preferred_element_type=F32)
    d1, d2 = m1 * by_lane, m2 * by_lane
    every = jnp.concatenate([d1, d2, m3, m1, m2], axis=0)
    high, low = split(every)
    row = iota(jnp.int32, (256, 80), 0) >> 3
    source = row + 6 * (row >= 10).astype(jnp.int32) + 6 * (row >= 20).astype(jnp.int32)
    source = jnp.where(row == 30, 48 + 9, jnp.where(row == 31, 64 + 9, source))
    up = (source == iota(jnp.int32, (256, 80), 1)).astype(BF16)
    column = iota(jnp.int32, (CZ, 240), 1)
    third = (column >= 80).astype(jnp.int32) + (column >= 160).astype(jnp.int32)
    across = (((column - 80 * third) >> 3) == iota(jnp.int32, (CZ, 240), 0)).astype(BF16)
    spread = [
        jnp.dot(
            jnp.dot(up, part, preferred_element_type=F32).astype(BF16),
            across,
            preferred_element_type=F32,
        )
        for part in (high, low)
    ]
    r, n = iota(jnp.int32, (256, 240), 0), iota(jnp.int32, (256, 240), 1)
    value = jnp.where(n < 160, spread[0], spread[1])
    matrix[...] = jnp.where((r & 7) == (n & 7), value, 0.0).astype(BF16)

    flame = flags[...].astype(F32)
    upper = (iota(jnp.int32, (CZ, CZ), 0) <= iota(jnp.int32, (CZ, CZ), 1)).astype(BF16)
    count = jnp.dot(flame.astype(BF16), upper, preferred_element_type=F32)
    total = jnp.dot(flame.astype(BF16), jnp.ones((CZ, CZ), BF16), preferred_element_type=F32)
    before = jnp.zeros((1, CZ), F32)
    keys = []
    for k in range(8):
        keys.append(count[k : k + 1] - 1.0 + before)
        before = before + total[k : k + 1]
    key = jnp.where(flame > 0.0, jnp.concatenate(keys, axis=0), -1.0)
    slot = iota(jnp.int32, (FMAX, CZ), 0).astype(F32)
    label = iota(jnp.int32, (8, CZ), 0)
    here = iota(jnp.int32, (8, CZ), 1).astype(F32)
    owner = owners[...].astype(F32)

    got = jnp.zeros((8, FMAX), F32)
    for k in range(8):
        hit = (slot == key[k : k + 1]).astype(BF16)
        facts = jnp.where(label == 0, here, jnp.where(label == 1, owner[k : k + 1], 1.0))
        facts = jnp.where(label == 3, float(k), facts)
        got = got + lax.dot_general(
            facts.astype(BF16), hit, (((1,), (1,)), ((), ())), preferred_element_type=F32
        )
    valid = got[2:3]
    index = got[3:4] * float(CZ) + got[0:1]
    who = got[1:2] + valid - 1.0
    zero = jnp.zeros((1, FMAX), F32)
    number = jnp.sum(valid, axis=1, keepdims=True) + zero
    below = [
        jnp.sum(jnp.where(index < at, valid, 0.0), axis=1, keepdims=True) + zero
        for at in (CH // 4, CH // 2, 3 * CH // 4)
    ]
    rows = [index, who, number] + below + [zero, zero]
    lists[...] = jnp.concatenate(rows, axis=0).astype(jnp.int32)


def halo_kernel(
    n_gx, n_gy, fields, diff, reaction, decay, flags, owners,
    cool, hot_out, heat, lists,
    hot, ext, mid, res, ov, taps, matrix, inverse, pad, where, first_t, terms, got, part, back,
    in_sem, send, recv, out_sem, list_sem, hot_sem, heat_send, heat_recv,
):
    gx, gy = lax.axis_index("gx"), lax.axis_index("gy")
    xm, xp = lax.rem(gx + n_gx - 1, n_gx), lax.rem(gx + 1, n_gx)
    ym, yp = lax.rem(gy + n_gy - 1, n_gy), lax.rem(gy + 1, n_gy)
    load = pltpu.make_async_copy(fields, ext.at[:, pl.ds(2, CX), pl.ds(8, CY), :], in_sem)
    load.start()
    targets = [
        (xp, gy), (xm, gy), (gx, yp), (gx, ym), (xp, yp), (xp, ym), (xm, yp), (xm, ym),
    ]
    barrier = pltpu.get_barrier_semaphore()
    for target in targets:
        pl.semaphore_signal(barrier, inc=1, device_id=target, device_id_type=MESH)
    planes = n_gy // 8
    plane = gy // 8
    place = gy - 8 * plane
    near_ones, far_ones = [], []
    for k in range(1, 8):
        other = place + k
        near_ones.append(jnp.where(other >= 8, other - 8, other))
    for k in range(1, planes):
        other = plane + k
        far_ones.append(jnp.where(other >= planes, other - planes, other))
    near_ids = [(gx, plane * 8 + other) for other in near_ones]
    far_ids = [(gx, other * 8 + place) for other in far_ones]
    for target in near_ids + far_ids:
        pl.semaphore_signal(barrier, inc=1, device_id=target, device_id_type=MESH)
    pl.semaphore_wait(barrier, 8 + 7 + planes - 1)
    jobs = []
    for first_c in range(0, COMP, GROUP):
        comps = (first_c, GROUP)
        jobs.append((xp, gy, comps, (CX - 2, 2), (0, CY), (0, 8)))
        jobs.append((xm, gy, comps, (0, 2), (0, CY), (CX + 2, 8)))
    faces = len(jobs)
    every = (0, COMP)
    jobs.append((gx, yp, every, (0, CX), (CY - 2, 2), (2, 6)))
    jobs.append((gx, ym, every, (0, CX), (0, 2), (2, CY + 8)))
    jobs.append((xp, yp, every, (CX - 1, 1), (CY - 1, 1), (1, 7)))
    jobs.append((xp, ym, every, (CX - 1, 1), (0, 1), (1, CY + 8)))
    jobs.append((xm, yp, every, (0, 1), (CY - 1, 1), (CX + 2, 7)))
    jobs.append((xm, ym, every, (0, 1), (0, 1), (CX + 2, CY + 8)))
    copies = []
    for number, (to_x, to_y, comps, xs, ys, (dx, dy)) in enumerate(jobs):
        copies.append(
            pltpu.make_async_remote_copy(
                src_ref=fields.at[pl.ds(*comps), pl.ds(*xs), pl.ds(*ys), :],
                dst_ref=ext.at[pl.ds(*comps), pl.ds(dx, xs[1]), pl.ds(dy, ys[1]), :],
                send_sem=send.at[number],
                recv_sem=recv.at[number],
                device_id=(to_x, to_y),
                device_id_type=MESH,
            )
        )
    for number in list(range(faces, faces + 2)) + list(range(faces)) + list(range(faces + 2, faces + 6)):
        copies[number].start()
    tables(reaction, decay, flags, owners, taps, matrix, inverse, lists, pad)
    listing = pltpu.make_async_copy(lists, where, list_sem)
    listing.start()
    load.wait()

    low_x, high_x = gx == 0, gx == n_gx - 1
    low_y, high_y = gy == 0, gy == n_gy - 1

    def lap(v, near):
        rows = v.shape[0]
        near = near + pltpu.roll(v, 1, 0) + pltpu.roll(v, rows - 1, 0)
        return near + jnp.dot(
            jnp.concatenate(split(v), axis=1), taps[...], preferred_element_type=F32
        )

    def masked(planes):
        top = jnp.where(low_y, 0.0, planes[:, 0:8])
        bottom = jnp.where(high_y, 0.0, planes[:, 8 + CY :])
        return jnp.concatenate([top, planes[:, 8 : 8 + CY], bottom], axis=1)

    def first(c, x, count):
        d = diff[c]
        shape = (count * CY, CZ)

        def rows(at):
            return ext[c, pl.ds(at, count), 8 : 8 + CY].reshape(shape)

        v = rows(x)
        new = v + d * lap(v, rows(x - 1) + rows(x + 1))
        mid[c, pl.ds(x - 1, count), 8 : 8 + CY] = new.reshape(count, CY, CZ)

    def rim(c, x, count):
        d = diff[c]

        def rows(at):
            both = [ext[c, pl.ds(at, count), 0:16], ext[c, pl.ds(at, count), CY : CY + 16]]
            return jnp.concatenate(both, axis=1).reshape(count * 32, CZ)

        v = rows(x)
        new = (v + d * lap(v, rows(x - 1) + rows(x + 1))).reshape(count, 32, CZ)
        to = pl.ds(x - 1, count)
        mid[c, to, 0:8] = jnp.where(low_y, 0.0, new[:, 0:8])
        mid[c, to, 8:9] = new[:, 8:9]
        mid[c, to, CY + 7 : CY + 8] = new[:, 23:24]
        mid[c, to, CY + 8 :] = jnp.where(high_y, 0.0, new[:, 24:32])

    def second(c, x, count):
        d = diff[c]
        shape = (count * 80, CZ)
        v = mid[c, pl.ds(x + 1, count)].reshape(shape)
        near = mid[c, pl.ds(x, count)].reshape(shape) + mid[c, pl.ds(x + 2, count)].reshape(shape)
        new = (v + d * lap(v, near)).reshape(count, 80, CZ)[:, 8 : 8 + CY]
        res[c, pl.ds(x * CY, count * CY)] = new.reshape(count * CY, CZ)

    def outer(cs):
        zero = jnp.zeros((80, CZ), F32)
        centre, near = [], []
        for c in cs:
            a, b, e, f = [ext[c, k] for k in range(4)]
            b = jnp.where(low_x, zero, b)
            centre += [b, e]
            near += [a + e, b + f]
            f, e, b, a = [ext[c, CX + k] for k in range(4)]
            b = jnp.where(high_x, zero, b)
            centre += [e, b]
            near += [f + b, e + a]
        centre = jnp.concatenate(centre, axis=0)
        total = lap(centre, jnp.concatenate(near, axis=0))
        centre2, near2 = [], []
        for k, c in enumerate(cs):
            part = slice(k * 320, k * 320 + 320)
            p = masked((centre[part] + diff[c] * total[part]).reshape(4, 80, CZ))
            m0 = jnp.where(low_x, zero, p[0])
            centre2 += [p[1], mid[c, 2]]
            near2 += [m0 + mid[c, 2], p[1] + mid[c, 3]]
            m1 = jnp.where(high_x, zero, p[3])
            centre2 += [mid[c, CX - 1], p[2]]
            near2 += [mid[c, CX - 2] + p[2], mid[c, CX - 1] + m1]
        centre2 = jnp.concatenate(centre2, axis=0)
        total2 = lap(centre2, jnp.concatenate(near2, axis=0))
        for k, c in enumerate(cs):
            part = slice(k * 320, k * 320 + 320)
            new = (centre2[part] + diff[c] * total2[part]).reshape(4, 80, CZ)[:, 8 : 8 + CY]
            res[c, 0 : 2 * CY] = new[0:2].reshape(2 * CY, CZ)
            res[c, (CX - 2) * CY :] = new[2:4].reshape(2 * CY, CZ)

    def clear(ref, xs, ys):
        @pl.loop(0, COMP)
        def _(c):
            ref[c, pl.ds(*xs), pl.ds(*ys), :] = jnp.zeros((xs[1], ys[1], CZ), F32)

    def edges(ref, xs):
        @pl.when(gy == 0)
        def _():
            clear(ref, xs, (0, 8))

        @pl.when(gy == n_gy - 1)
        def _():
            clear(ref, xs, (CY + 8, 8))

    @pl.loop(0, COMP)
    def _(c):
        first(c, 3, 7)
        first(c, 10, 7)

    copies[faces].wait_recv()
    copies[faces + 1].wait_recv()
    edges(ext, (2, CX))

    @pl.loop(0, COMP)
    def _(c):
        rim(c, 3, 14)

    @pl.loop(0, COMP)
    def _(c):
        second(c, 2, 6)
        second(c, 8, 6)

    inv = inverse[...]
    inv = jnp.concatenate([inv, inv], axis=1)

    def cool_tile(t):
        at = [t * 16 + w * 8 for w in range(2)]
        if not isinstance(t, int):
            at = [pl.multiple_of(a, 8) for a in at]
        groups = [
            jnp.concatenate([res[c, pl.ds(a, 8), :] for c in range(COMP)], axis=0) for a in at
        ]
        rows = substep(jnp.concatenate(groups, axis=1), matrix[...], inv)
        for w in range(2):
            for c in range(COMP):
                ov[c, pl.ds(at[w], 8), :] = rows[c][:, w * CZ : (w + 1) * CZ]

    edge = 2 * CY // 16
    inner = CH // 16 - 2 * edge

    @pl.loop(0, inner // 12)
    def _(k):
        for t in range(12):
            cool_tile(edge + k * 12 + t)

    def store(k, start, size):
        where_to = pl.ds(start, size)
        return pltpu.make_async_copy(ov.at[:, where_to, :], cool.at[:, where_to, :], out_sem.at[k])

    stores = [
        store(0, 2 * CY, (CX - 4) * CY), store(1, 0, 2 * CY), store(2, (CX - 2) * CY, 2 * CY),
    ]
    stores[0].start()

    for number in range(faces + 2, faces + 6):
        copies[number].wait_recv()
    edges(ext, (1, 1))
    edges(ext, (CX + 2, 1))

    for group in range(faces // 2):
        copies[2 * group].wait_recv()
        copies[2 * group + 1].wait_recv()
        cs = list(range(group * GROUP, (group + 1) * GROUP))
        outer(cs)

    listing.wait()

    @pl.loop(0, FMAX // 8)
    def _(g):
        for r in range(8):
            at = jnp.clip(where[0, g * 8 + r], 0, CH - 1)
            for c in range(COMP):
                hot[g, pl.ds(c * 8 + r, 1), :] = res[c, pl.ds(at, 1), :]
        first_t[g] = hot[g, 72:80, :]

    @pl.loop(0, FLAME_SUB)
    def _(s):
        for t in range(FMAX // 16):
            flame_tile(hot, t, matrix, inv)

    leaving = pltpu.make_async_copy(hot, hot_out, hot_sem)
    leaving.start()
    gain = (hot[:, 72:80, :] - first_t[...]).reshape(FMAX, CZ)
    row = lax.broadcasted_iota(jnp.int32, (64, FMAX), 0)
    owner = jnp.where((row & 7) < planes, (row & 7) * 8 + (row >> 3), -2)
    onehot = (owner == lists[1:2, :]).astype(BF16)
    total = jnp.zeros((64, CZ), F32)
    for piece in split(gain):
        total = total + jnp.dot(onehot, piece, preferred_element_type=F32)
    terms[...] = total.reshape(8, 8, CZ)

    sums = []
    for k, (other, target) in enumerate(zip(near_ones, near_ids)):
        copy = pltpu.make_async_remote_copy(
            src_ref=terms.at[other],
            dst_ref=got.at[k],
            send_sem=heat_send.at[k],
            recv_sem=heat_recv.at[k],
            device_id=target,
            device_id_type=MESH,
        )
        copy.start()
        sums.append(copy)
    for t in range(edge):
        cool_tile(t)
    stores[1].start()
    total = terms[place]
    for k in range(7):
        sums[k].wait_recv()
        total = total + got[k]
    part[...] = total
    for k, target in enumerate(far_ids):
        copy = pltpu.make_async_remote_copy(
            src_ref=part,
            dst_ref=back.at[k],
            send_sem=heat_send.at[7 + k],
            recv_sem=heat_recv.at[7 + k],
            device_id=target,
            device_id_type=MESH,
        )
        copy.start()
        sums.append(copy)
    for t in range(edge):
        cool_tile(edge + inner + t)
    stores[2].start()
    for k in range(planes - 1):
        sums[7 + k].wait_recv()
        total = total + back[k]
    total = jnp.where(lax.broadcasted_iota(jnp.int32, (8, CZ), 0) == plane, total, 0.0)
    total = jnp.sum(jnp.sum(total, axis=0, keepdims=True), axis=1, keepdims=True)
    heat[...] = total * (1.0 / math.sqrt(CZ) / math.sqrt(RMAX))
    for copy in copies + sums:
        copy.wait_send()
    leaving.wait()
    for copy in stores:
        copy.wait()


def sigmoid(x):
    return 0.5 * jnp.tanh(0.5 * x) + 0.5


def substep(state, matrix, inverse):
    high, low = split(state)
    r = jnp.dot(matrix, jnp.concatenate([high, low, high], axis=0), preferred_element_type=F32)
    last = state[72:80]
    base = last * inverse[72:80]
    g0 = sigmoid(last)
    g1 = sigmoid(base + g0 * r[240:248])
    g2 = sigmoid(base + g1 * (r[72:80] + g0 * r[248:256]))
    rows = []
    for c in range(COMP):
        at = 8 * c
        inner = r[80 + at : 88 + at] + g0 * r[160 + at : 168 + at]
        rows.append(state[at : at + 8] * inverse[at : at + 8] + g2 * (r[at : at + 8] + g1 * inner))
    return rows


def flame_tile(cur, t, matrix, inv):
    rows = substep(jnp.concatenate([cur[2 * t], cur[2 * t + 1]], axis=1), matrix[...], inv)
    new = jnp.concatenate(rows, axis=0)
    cur[2 * t] = new[:, :CZ]
    cur[2 * t + 1] = new[:, CZ:]


def merge_kernel(cool, hot_in, index, out, ov, hot, in_sem, hot_sem, out_sem):
    quarter = CH // 4

    def fetch(k):
        at = pl.ds(k * quarter, quarter)
        return pltpu.make_async_copy(cool.at[:, at, :], ov.at[:, at, :], in_sem.at[k])

    def flush(k):
        at = pl.ds(k * quarter, quarter)
        return pltpu.make_async_copy(ov.at[:, at, :], out.at[:, at, :], out_sem.at[k])

    flames = pltpu.make_async_copy(hot_in, hot, hot_sem)
    fetch(0).start()
    flames.start()
    for k in range(1, 4):
        fetch(k).start()
    flames.wait()
    start = 0
    for k in range(4):
        stop = jnp.clip(index[3 + k, 0] if k < 3 else index[2, 0], 0, FMAX)
        fetch(k).wait()

        @pl.loop(0, (jnp.maximum(stop - start, 0) + 7) // 8)
        def _(g, start=start, stop=stop):
            for r in range(8):
                p = jnp.minimum(start + g * 8 + r, stop - 1)
                at = index[0, p]
                for c in range(COMP):
                    ov[c, pl.ds(at, 1), :] = hot[p >> 3, pl.ds(c * 8 + (p & 7), 1), :]

        start = stop
        flush(k).start()
    for k in range(4):
        flush(k).wait()


def per_device(n_gx, n_gy, fields, diffusivity, decay_rates, reaction_matrix, owner_index, flame_flag):
    shape = (COMP, CH, CZ)
    groups = FMAX // 8
    faces = 2 * (COMP // GROUP)
    partners = 7 + n_gy // 8 - 1
    dma = pltpu.SemaphoreType.DMA
    as_f32 = lambda *dims: jax.ShapeDtypeStruct(dims, F32)
    cool, hot, heat, lists = pl.pallas_call(
        functools.partial(halo_kernel, n_gx, n_gy),
        out_shape=(
            as_f32(*shape),
            as_f32(groups, 80, CZ),
            as_f32(1, 1),
            jax.ShapeDtypeStruct((8, FMAX), jnp.int32),
        ),
        in_specs=[ANY, SMEM, VMEM, SMEM, VMEM, VMEM],
        out_specs=(ANY, ANY, VMEM, VMEM),
        scratch_shapes=[
            pltpu.VMEM((groups, 80, CZ), F32),
            pltpu.VMEM((COMP, CX + 4, CY + 16, CZ), F32),
            pltpu.VMEM((COMP, CX + 2, CY + 16, CZ), F32),
            pltpu.VMEM(shape, F32),
            pltpu.VMEM(shape, F32),
            pltpu.VMEM((2 * CZ, CZ), BF16),
            pltpu.VMEM((256, 240), BF16),
            pltpu.VMEM((80, CZ), F32),
            pltpu.VMEM((CZ, CZ), F32),
            pltpu.SMEM((8, FMAX), jnp.int32),
            pltpu.VMEM((groups, 8, CZ), F32),
            pltpu.VMEM((8, 8, CZ), F32),
            pltpu.VMEM((7, 8, CZ), F32),
            pltpu.VMEM((8, CZ), F32),
            pltpu.VMEM((n_gy // 8 - 1, 8, CZ), F32),
            dma,
            dma((faces + 6,)),
            dma((faces + 6,)),
            dma((3,)),
            dma,
            dma,
            dma((partners,)),
            dma((partners,)),
        ],
        compiler_params=pltpu.CompilerParams(
            collective_id=0, has_side_effects=True, vmem_limit_bytes=LIMIT
        ),
        name="halo_diffuse_react",
    )(
        fields, diffusivity, reaction_matrix, decay_rates,
        flame_flag.reshape(8, CZ), owner_index.reshape(8, CZ),
    )
    merged = pl.pallas_call(
        merge_kernel,
        out_shape=as_f32(*shape),
        in_specs=[ANY, ANY, SMEM],
        out_specs=ANY,
        scratch_shapes=[
            pltpu.VMEM(shape, F32),
            pltpu.VMEM((groups, 80, CZ), F32),
            dma((4,)),
            dma,
            dma((4,)),
        ],
        compiler_params=pltpu.CompilerParams(vmem_limit_bytes=LIMIT),
        name="merge_flames",
    )(cool, hot, lists)
    return merged.reshape(COMP, CX, CY, CZ), heat


def solution(mesh):
    return jax.shard_map(
        functools.partial(per_device, mesh.shape["gx"], mesh.shape["gy"]),
        mesh=mesh,
        in_specs=(
            P(None, "gx", "gy", None),
            P(),
            P(),
            P(),
            P("gx", "gy", None),
            P("gx", "gy", None),
        ),
        out_specs=(P(None, "gx", "gy", None), P("gx", "gy")),
        check_vma=False,
    )
```

profile of v0, /device:TPU:1, one launch (start us, length us, event | category | flops | bytes accessed | tf_op | source)
XLA Modules:
  0.0 53.1 jit_solution(7465790870806160430)
XLA Ops:
  0.6 45.0 %halo_diffuse_react.1 = (f32[10,1024,128]{2,1,0:T(8,128)}, f32[32,80,128]{2,1,0:T(8,128)}, f32[1,1]{1,0:T(1,128)}, s32[8,256]{1,0:T(8,128)}) custom-call(f32[10,16,64,128]{3,2,1,0:T(8,128)} %fields.1, f32[10]{0:T(128)} %diff.1, f32[10,10]{1,0:T(8,128)} %reaction.1, f32[10]{0:T(128)} %decay.1, s32[8,128]{1,0:T(8,128)} %bitcast.4, s32[8,128]{1,0:T(8,128)} %bitcast.5), custom_call_target="tpu_custom_call" | custom-call | tf_op jit(solution)/shard_map/halo_diffuse_react/pallas_call | solution.py:479
  45.6 5.8 %merge_flames.1 = f32[10,1024,128]{2,1,0:T(8,128)} custom-call(f32[10,1024,128]{2,1,0:T(8,128)} %get-tuple-element.6.cool, f32[32,80,128]{2,1,0:T(8,128)} %get-tuple-element.7.hot_in, s32[8,256]{1,0:T(8,128)} %get-tuple-element.8.index), custom_call_target="tpu_custom_call" | custom-call | tf_op jit(solution)/shard_map/merge_flames/pallas_call | solution.py:522
where the time goes:
time: 53.4 us; the launch traced here: 53.1 us
  Pallas kernels  50.8 us (95%)
  between operations  2.35 us (4%)
    pallas_call x1, Pallas kernels, per_device(): pl.pallas_call(functools.partial(halo_kernel, n_gx, n_gy), out_shape=(as_...  45 us
    pallas_call x1, Pallas kernels, per_device(): pl.pallas_call(merge_kernel, out_shape=as_f32(*shape), in_specs=[ANY, ANY...  5.83 us

commit v1 on v0

--- a/solution.py
+++ b/solution.py
@@ -15,7 +15,7 @@
 CH = CX * CY
 FMAX = 256
 RMAX = 60
-GROUP = 2
+GROUP = 5
 
 F32, BF16 = jnp.float32, jnp.bfloat16
 MESH = pl.DeviceIdType.MESH

time: 53.4 us -> 53.1 us (level); the launches traced: 53.1 us -> 52.2 us
  Pallas kernels: 50.8 us -> 49.9 us
    pallas_call x1, Pallas kernels: 45 us -> 44.1 us  [per_device(): pl.pallas_call(functools.partial(halo_kernel, n_gx, n_gy), out_shape=(as_...]
where the time goes in v1:
time: 53.1 us; the launch traced here: 52.2 us
  Pallas kernels  49.9 us (94%)
  between operations  2.35 us (4%)
    pallas_call x1, Pallas kernels, per_device(): pl.pallas_call(functools.partial(halo_kernel, n_gx, n_gy), out_shape=(as_...  44.1 us
    pallas_call x1, Pallas kernels, per_device(): pl.pallas_call(merge_kernel, out_shape=as_f32(*shape), in_specs=[ANY, ANY...  5.76 us

profile of v1, /device:TPU:1, one launch (start us, length us, event | category | flops | bytes accessed | tf_op | source)
XLA Modules:
  0.0 52.2 jit_solution(3815870014488540627)
XLA Ops:
  0.6 44.1 %halo_diffuse_react.1 = (f32[10,1024,128]{2,1,0:T(8,128)}, f32[32,80,128]{2,1,0:T(8,128)}, f32[1,1]{1,0:T(1,128)}, s32[8,256]{1,0:T(8,128)}) custom-call(f32[10,16,64,128]{3,2,1,0:T(8,128)} %fields.1, f32[10]{0:T(128)} %diff.1, f32[10,10]{1,0:T(8,128)} %reaction.1, f32[10]{0:T(128)} %decay.1, s32[8,128]{1,0:T(8,128)} %bitcast.4, s32[8,128]{1,0:T(8,128)} %bitcast.5), custom_call_target="tpu_custom_call" | custom-call | tf_op jit(solution)/shard_map/halo_diffuse_react/pallas_call | solution.py:479
  44.7 5.8 %merge_flames.1 = f32[10,1024,128]{2,1,0:T(8,128)} custom-call(f32[10,1024,128]{2,1,0:T(8,128)} %get-tuple-element.6.cool, f32[32,80,128]{2,1,0:T(8,128)} %get-tuple-element.7.hot_in, s32[8,256]{1,0:T(8,128)} %get-tuple-element.8.index), custom_call_target="tpu_custom_call" | custom-call | tf_op jit(solution)/shard_map/merge_flames/pallas_call | solution.py:522

commit v2 on v1

--- a/solution.py
+++ b/solution.py
@@ -343,9 +343,9 @@
                 hot[g, pl.ds(c * 8 + r, 1), :] = res[c, pl.ds(at, 1), :]
         first_t[g] = hot[g, 72:80, :]
 
-    @pl.loop(0, FLAME_SUB)
+    @pl.loop(0, FLAME_SUB // 2)
     def _(s):
-        for t in range(FMAX // 16):
+        for t in list(range(FMAX // 16)) * 2:
             flame_tile(hot, t, matrix, inv)
 
     leaving = pltpu.make_async_copy(hot, hot_out, hot_sem)

time: 53.1 us -> 52.2 us (0.983)
  Pallas kernels: 49.9 us -> 49.3 us
    pallas_call x1, Pallas kernels: 44.1 us -> 43.5 us  [per_device(): pl.pallas_call(functools.partial(halo_kernel, n_gx, n_gy), out_shape=(as_...]
where the time goes in v2:
time: 52.2 us; the launch traced here: 51.6 us
  Pallas kernels  49.3 us (94%)
  between operations  2.35 us (5%)
    pallas_call x1, Pallas kernels, per_device(): pl.pallas_call(functools.partial(halo_kernel, n_gx, n_gy), out_shape=(as_...  43.5 us
    pallas_call x1, Pallas kernels, per_device(): pl.pallas_call(merge_kernel, out_shape=as_f32(*shape), in_specs=[ANY, ANY...  5.76 us

profile of v2, /device:TPU:1, one launch (start us, length us, event | category | flops | bytes accessed | tf_op | source)
XLA Modules:
  0.0 51.6 jit_solution(9684198549483804126)
XLA Ops:
  0.6 43.5 %halo_diffuse_react.1 = (f32[10,1024,128]{2,1,0:T(8,128)}, f32[32,80,128]{2,1,0:T(8,128)}, f32[1,1]{1,0:T(1,128)}, s32[8,256]{1,0:T(8,128)}) custom-call(f32[10,16,64,128]{3,2,1,0:T(8,128)} %fields.1, f32[10]{0:T(128)} %diff.1, f32[10,10]{1,0:T(8,128)} %reaction.1, f32[10]{0:T(128)} %decay.1, s32[8,128]{1,0:T(8,128)} %bitcast.4, s32[8,128]{1,0:T(8,128)} %bitcast.5), custom_call_target="tpu_custom_call" | custom-call | tf_op jit(solution)/shard_map/halo_diffuse_react/pallas_call | solution.py:479
  44.1 5.8 %merge_flames.1 = f32[10,1024,128]{2,1,0:T(8,128)} custom-call(f32[10,1024,128]{2,1,0:T(8,128)} %get-tuple-element.6.cool, f32[32,80,128]{2,1,0:T(8,128)} %get-tuple-element.7.hot_in, s32[8,256]{1,0:T(8,128)} %get-tuple-element.8.index), custom_call_target="tpu_custom_call" | custom-call | tf_op jit(solution)/shard_map/merge_flames/pallas_call | solution.py:522
